TPU v7x, 32 devices: a whole 2x2x4 slice. The times are simulated.
32 devices in a mesh: groups: 2 (over y), seq: 4 (over z), mp: 2 (over x), branch: 2 (over core).
Axes of the slice: x: 2, y: 2, z: 4, core: 2. Of those that a mesh axis runs over, the one named last changes fastest.
Arguments:
- streams: float32 [2, 8, 256, 1152], P('branch', ('groups', 'seq')), parts along dimension 1, may hold values from -6 to 6
- modulation: float32 [2, 6, 1152], P('branch'), may hold values from -3 to 3
- s_qkv: bfloat16 [2, 1152, 3, 1152], P('branch', 'seq', None, 'mp'), may hold values from -0.1875 to 0.1875
- s_out: bfloat16 [2, 1152, 1152], P('branch', 'mp', 'seq'), may hold values from -0.25 to 0.25
- w_in: bfloat16 [2, 1152, 4608], P('branch', 'seq', 'mp'), may hold values from -0.1875 to 0.1875
- w_out: bfloat16 [2, 4608, 1152], P('branch', 'mp', 'seq'), may hold values from -0.125 to 0.125
- hint_gain: float32 [13, 1152], replicated, may hold values from 0.3 to 3
- inject_layer: int32 [4], replicated, may hold values from 0 to 12
- hint_weight: bfloat16 [1152, 1152], P('seq', 'mp'), may hold values from -0.1875 to 0.1875
- t_mod: float32 [3, 1152], replicated, may hold values from -3 to 3
- t_qkv: bfloat16 [1152, 3, 1152], P('seq', None, 'mp'), may hold values from -0.1875 to 0.1875
- t_out: bfloat16 [1152, 1152], P('mp', 'seq'), may hold values from -0.25 to 0.25
Outputs:
- main_out: float32 [8, 256, 1152], P('groups', ('seq', 'branch'), 'mp'), parts along dimension 0
There are 2 independent parts, one for each index of `groups`. A program takes and returns all parts, laid end to end along the dimension named above; an argument that names none is the same for every part. Nothing has to cross between parts.
All inputs are finite; a program needn't handle non-finite values.
Results may differ from a plain program's by a relative error of at most 0.014.
Values may be sent and summed in bfloat16 or wider, within the bound.
A program may use at most 64 MiB of HBM per device.

v0:
```python
import jax
import jax.numpy as jnp
from jax import lax
from jax.sharding import PartitionSpec as P

D = 1152
HEAD_DIM = 72
HINT_LAYERS = 13


def layer_norm(value, shift, scale):
    mean = jnp.mean(value, axis=-1, keepdims=True)
    centred = value - mean
    var = jnp.mean(centred * centred, axis=-1, keepdims=True)
    return centred * lax.rsqrt(var + 1e-06) * (1.0 + scale) + shift


def attend(query, keys, values):
    scores = jnp.einsum("qhd,khd->hqk", query, keys, precision=lax.Precision.HIGHEST) / jnp.sqrt(
        jnp.float32(HEAD_DIM)
    )
    weights = jnp.exp(scores)
    weights = weights / jnp.sum(weights, axis=-1, keepdims=True)
    result = jnp.einsum("hqk,khd->qhd", weights, values, precision=lax.Precision.HIGHEST)
    return result.reshape(result.shape[0], -1)


def row_product(left, piece):
    return jnp.dot(left, piece, preferred_element_type=jnp.float32)


def on_device(
    streams,
    modulation,
    s_qkv,
    s_out,
    w_in,
    w_out,
    hint_gain,
    inject_layer,
    hint_weight,
    t_mod,
    t_qkv,
    t_out,
):
    stream = streams[0, 0]
    mods = modulation[0]
    tokens = stream.shape[0]
    quarter = s_qkv.shape[3]
    offset = lax.axis_index("mp") * quarter
    local_heads = quarter // HEAD_DIM

    def share(vector):
        return lax.dynamic_slice_in_dim(vector, offset, quarter, 0)

    normed = layer_norm(stream, mods[0], mods[1]).astype(jnp.bfloat16)
    piece = lax.all_gather(s_qkv, "seq", axis=1, tiled=True)
    qkv = row_product(normed, piece[0].reshape(piece.shape[1], 3 * quarter))
    qkv = qkv.reshape(tokens, 3, local_heads, HEAD_DIM)
    attended = attend(qkv[:, 0], qkv[:, 1], qkv[:, 2]).astype(jnp.bfloat16)
    projected = jnp.dot(
        attended,
        lax.all_gather(s_out, "seq", axis=2, tiled=True)[0],
        preferred_element_type=jnp.float32,
    )
    partial_value = lax.psum_scatter(
        projected.astype(jnp.bfloat16), "mp", scatter_dimension=1, tiled=True
    ).astype(jnp.float32)
    stream_share = (
        lax.dynamic_slice_in_dim(stream, offset, quarter, 1) + share(mods[2]) * partial_value
    )
    stream = lax.all_gather(stream_share.astype(jnp.bfloat16), "mp", axis=1, tiled=True).astype(
        stream_share.dtype
    )
    normed = layer_norm(stream, mods[3], mods[4]).astype(jnp.bfloat16)
    upward = row_product(normed, lax.all_gather(w_in, "seq", axis=1, tiled=True)[0])
    hidden = jax.nn.gelu(upward, approximate=True).astype(jnp.bfloat16)
    downward = jnp.dot(
        hidden,
        lax.all_gather(w_out, "seq", axis=2, tiled=True)[0],
        preferred_element_type=jnp.float32,
    )
    mlp_part = lax.psum_scatter(
        downward.astype(jnp.bfloat16), "mp", scatter_dimension=1, tiled=True
    ).astype(jnp.float32)
    section_out = stream_share + share(mods[5]) * mlp_part
    moved = lax.all_to_all(
        lax.all_to_all(
            section_out[None, None].astype(jnp.bfloat16),
            "seq",
            split_axis=2,
            concat_axis=1,
            tiled=True,
        ),
        "branch",
        split_axis=2,
        concat_axis=0,
        tiled=True,
    ).astype(jnp.float32)
    frames = moved.shape[1]
    positions = moved.shape[2]
    rows = frames * positions
    control = moved[0]
    main_share = moved[1].reshape(rows, quarter)
    picks = (inject_layer[:, None] == jnp.arange(HINT_LAYERS, dtype=jnp.int32)[None, :]).astype(
        jnp.float32
    )
    gain = jnp.sum(picks[:, :, None] * hint_gain[None, :, :], axis=1)
    control_whole = lax.all_gather(control.astype(jnp.bfloat16), "mp", axis=2, tiled=True).astype(
        control.dtype
    )
    hint_in = (control_whole * gain[:, None, :]).astype(jnp.bfloat16).reshape(rows, D)
    hint = row_product(hint_in, lax.all_gather(hint_weight, "seq", axis=0, tiled=True))
    joined_share = main_share + hint
    joined = lax.all_gather(joined_share.astype(jnp.bfloat16), "mp", axis=1, tiled=True).astype(
        joined_share.dtype
    )
    normed_t = layer_norm(joined, t_mod[0], t_mod[1]).astype(jnp.bfloat16)
    piece = lax.all_gather(t_qkv, "seq", axis=0, tiled=True)
    tqkv = row_product(normed_t, piece.reshape(piece.shape[0], 3 * quarter))
    tqkv = tqkv.reshape(frames, positions, 3, local_heads, HEAD_DIM).transpose(1, 0, 2, 3, 4)
    attended_t = jax.vmap(attend)(tqkv[:, :, 0], tqkv[:, :, 1], tqkv[:, :, 2])
    attended_t = attended_t.transpose(1, 0, 2).reshape(rows, quarter).astype(jnp.bfloat16)
    projected_t = jnp.dot(
        attended_t,
        lax.all_gather(t_out, "seq", axis=1, tiled=True),
        preferred_element_type=jnp.float32,
    )
    temporal_part = lax.psum_scatter(
        projected_t.astype(jnp.bfloat16), "mp", scatter_dimension=1, tiled=True
    ).astype(jnp.float32)
    result = joined_share + share(t_mod[2]) * temporal_part
    return result.reshape(frames, positions, quarter)


def solution(mesh):
    in_specs = (
        P("branch", ("groups", "seq"), None, None),
        P("branch", None, None),
        P("branch", "seq", None, "mp"),
        P("branch", "mp", "seq"),
        P("branch", "seq", "mp"),
        P("branch", "mp", "seq"),
        P(),
        P(),
        P("seq", "mp"),
        P(),
        P("seq", None, "mp"),
        P("mp", "seq"),
    )
    out_specs = P("groups", ("seq", "branch"), "mp")
    return jax.shard_map(
        on_device, mesh=mesh, in_specs=in_specs, out_specs=out_specs, check_vma=False
    )
```

profile of v0, /device:TPU:0, one launch (start us, length us, event | category | flops | bytes accessed | tf_op | source)
XLA Modules:
  0.0 556.6 jit_solution(1745419225290000428)
XLA Ops:
  6.5 0.7 all-gather.9.cloned.1.call-update
  7.3 0.7 all-gather.11.cloned.1.call-update
  8.1 0.1 reduce_sum.81
  8.2 0.3 fusion.34
  8.6 87.6 %all-gather.9.cloned.1.call-done = bf16[1,1152,3,576]{3,1,2,0:T(8,128)(2,1)} async-done(((bf16[1,288,3,576]{3,1,2,0:T(8,128)(2,1)}), bf16[1,1152,3,576]{3,1,2,0:T(8,128)(2,1)}) %all-gather.9.cloned.1.call-update) | async-done | bytes 3981328 | tf_op jit(solution)/shard_map/all_gather | solution.py:57
  96.2 6.6 %copy.53 = bf16[1,1152,3,576]{1,3,2,0:T(8,128)(2,1)} copy(bf16[1,1152,3,576]{3,1,2,0:T(8,128)(2,1)} %all-gather.9.cloned.1.call-done) | data formatting | bytes 7962624 | tf_op jit(solution)/shard_map/all_gather | solution.py:57
  102.8 3.8 fusion.45
  106.6 2.1 fusion.21
  108.7 1.7 fusion.26
  110.4 21.4 %all-gather.11.cloned.1.call-done = bf16[1,576,1152]{1,2,0:T(8,128)(2,1)} async-done(((bf16[1,576,288]{1,2,0:T(8,128)(2,1)}), bf16[1,576,1152]{1,2,0:T(8,128)(2,1)}) %all-gather.11.cloned.1.call-update) | async-done | bytes 1327120 | tf_op jit(solution)/shard_map/all_gather | solution.py:63
  131.8 2.8 convolution_convert_fusion
  134.7 0.5 all-gather.13.cloned.1.call-update
  135.3 0.5 all-gather.15.cloned.1.call-update
  135.9 0.2 constant_dynamic-slice_fusion
  136.1 0.2 copy.52
  136.3 0.1 dynamic-slice_reduce_fusion.2
  136.4 12.5 %reduce-scatter.4.cloned.1.call-done = bf16[256,576]{0,1:T(8,128)(2,1)} async-done(((bf16[256,1152]{0,1:T(8,128)(2,1)}), bf16[256,576]{0,1:T(8,128)(2,1)}) %reduce-scatter.4.cloned.1.call-update) | async-done | bytes 294928 | tf_op jit(solution)/shard_map/reduce_scatter | solution.py:66
  148.9 1.1 fusion.70
  150.1 9.4 %all_gather.32 = bf16[256,1152]{0,1:T(8,128)(2,1)S(1)} all-gather(bf16[256,576]{0,1:T(8,128)(2,1)S(1)} %fusion.70), channel_id=1, replica_groups=mesh['groups'=2,'seq'=4,'mp'=2,'branch'=2] {'mp'}, dimensions={1}, use_global_device_ids=true | all-gather | bytes 884736 | tf_op jit(solution)/shard_map/all_gather | solution.py:72
  159.5 0.2 convert_reduce_fusion
  159.7 0.2 fusion.29
  159.9 89.8 %all-gather.13.cloned.1.call-done = bf16[1,1152,2304]{2,1,0:T(8,128)(2,1)} async-done(((bf16[1,288,2304]{2,1,0:T(8,128)(2,1)}), bf16[1,1152,2304]{2,1,0:T(8,128)(2,1)}) %all-gather.13.cloned.1.call-update) | async-done | bytes 5308432 | tf_op jit(solution)/shard_map/all_gather | solution.py:76
  249.6 99.0 %all-gather.15.cloned.1.call-done = bf16[1,2304,1152]{1,2,0:T(8,128)(2,1)} async-done(((bf16[1,2304,288]{1,2,0:T(8,128)(2,1)}), bf16[1,2304,1152]{1,2,0:T(8,128)(2,1)}) %all-gather.15.cloned.1.call-update) | async-done | bytes 5308432 | tf_op jit(solution)/shard_map/all_gather | solution.py:80
  348.7 8.2 %fusion.4 = bf16[256,1152]{0,1:T(8,128)(2,1)} fusion(bf16[1,2304,1152]{1,2,0:T(8,128)(2,1)} %all-gather.15.cloned.1.call-done, bf16[1,1152,2304]{2,1,0:T(8,128)(2,1)} %all-gather.13.cloned.1.call-done, bf16[256,1152]{0,1:T(8,128)(2,1)S(1)} %all_gather.32, f32[1152]{0:T(1024)S(1)} %get-tuple-element.18, f32[1152]{0:T(1024)S(1)} %get-tuple-element.21, ...), kind=kOutput, calls=%fused_computation.6 | convolution fusion | flops 2725281792 | bytes 11807744 | tf_op jit(solution)/shard_map/dot_general | solution.py:78
  357.0 0.7 all-gather.19.cloned.1.call-update
  357.7 0.7 all-gather.17.cloned.1.call-update
  358.4 0.2 all-gather.21.cloned.1.call-start
  358.7 0.5 all-gather.21.cloned.1.call-update
  359.2 0.1 dynamic-slice_reduce_fusion.1
  359.3 11.5 %reduce-scatter.6.cloned.1.call-done = bf16[256,576]{0,1:T(8,128)(2,1)} async-done(((bf16[256,1152]{0,1:T(8,128)(2,1)}), bf16[256,576]{0,1:T(8,128)(2,1)}) %reduce-scatter.6.cloned.1.call-update) | async-done | bytes 294928 | tf_op jit(solution)/shard_map/reduce_scatter | solution.py:83
  370.7 1.2 fusion.71
  371.9 0.6 copy.55
  372.5 0.5 broadcast.136
  373.1 2.7 reduce.19
  375.8 1.1 reshape.175
  376.9 4.6 all-to-all-start
  381.5 0.1 multiply_reduce_fusion
  381.7 81.2 %all-gather.19.cloned.1.call-done = bf16[1152,3,576]{2,0,1:T(8,128)(2,1)} async-done(((bf16[288,3,576]{2,0,1:T(8,128)(2,1)}), bf16[1152,3,576]{2,0,1:T(8,128)(2,1)}) %all-gather.19.cloned.1.call-update) | async-done | bytes 3981328 | tf_op jit(solution)/shard_map/all_gather | solution.py:119
  462.9 6.6 %copy.62 = bf16[1152,3,576]{0,2,1:T(8,128)(2,1)} copy(bf16[1152,3,576]{2,0,1:T(8,128)(2,1)} %all-gather.19.cloned.1.call-done) | data formatting | bytes 7962624 | tf_op jit(solution)/shard_map/all_gather | solution.py:119
  469.4 0.6 reshape.176
  470.1 0.3 copy.56
  470.3 4.0 all_to_all.21
  474.4 0.3 copy.58
  474.8 16.1 %all-gather = bf16[1,1,4,32,1152]{3,2,1,0,4:T(4,128)(2,1)S(1)} all-gather(bf16[1,1,4,32,576]{3,2,1,0,4:T(4,128)(2,1)S(1)} %copy.58), channel_id=2, replica_groups=mesh['groups'=2,'seq'=4,'mp'=2,'branch'=2] {'mp'}, dimensions={4}, use_global_device_ids=true | all-gather | bytes 442368 | tf_op jit(solution)/shard_map/all_gather | solution.py:109
  490.8 1.2 copy.59
  492.1 0.1 copy.60
  492.3 5.9 %all-gather.17.cloned.1.call-done = bf16[1152,576]{1,0:T(8,128)(2,1)} async-done(((bf16[288,576]{1,0:T(8,128)(2,1)}), bf16[1152,576]{1,0:T(8,128)(2,1)}) %all-gather.17.cloned.1.call-update) | async-done | bytes 1327120 | tf_op jit(solution)/shard_map/all_gather | solution.py:113
  498.2 2.0 fusion.83
  500.2 6.0 %all_gather.37 = bf16[128,1152]{0,1:T(8,128)(2,1)S(1)} all-gather(bf16[128,576]{0,1:T(8,128)(2,1)S(1)} %get-tuple-element.25), channel_id=1, replica_groups=mesh['groups'=2,'seq'=4,'mp'=2,'branch'=2] {'mp'}, dimensions={1}, use_global_device_ids=true | all-gather | bytes 442368 | tf_op jit(solution)/shard_map/all_gather | solution.py:115
  506.2 0.2 convert_reduce_fusion.1
  506.4 0.2 fusion.40
  506.6 0.4 fusion.43
  507.0 0.2 copy.61
  507.2 4.3 convolution_bitcast_fusion
  511.5 0.1 slice_bitcast_fusion.7
  511.6 2.5 fusion.25
  514.2 2.6 fusion.35
  516.8 0.2 convert_element_type.127
  517.0 17.1 %all-gather.21.cloned.1.call-done = bf16[576,1152]{0,1:T(8,128)(2,1)} async-done(((bf16[576,288]{0,1:T(8,128)(2,1)}), bf16[576,1152]{0,1:T(8,128)(2,1)}) %all-gather.21.cloned.1.call-update) | async-done | bytes 1327120 | tf_op jit(solution)/shard_map/all_gather | solution.py:126
  534.1 2.6 convolution_convert_fusion.1
  536.8 0.1 dynamic-slice_reduce_fusion
  536.9 11.0 %reduce-scatter.8.cloned.1.call-done = bf16[128,576]{0,1:T(8,128)(2,1)} async-done(((bf16[128,1152]{0,1:T(8,128)(2,1)}), bf16[128,576]{0,1:T(8,128)(2,1)}) %reduce-scatter.8.cloned.1.call-update) | async-done | bytes 147472 | tf_op jit(solution)/shard_map/reduce_scatter | solution.py:129
  547.8 1.0 multiply_add_fusion
  548.9 0.9 copy.68
  (40 shorter events, 0.7 us)
Async XLA Ops:
  6.5 1.5 copy-start
  6.5 89.7 %all-gather.9.cloned.1.call-start = ((), (), s32[]{:S(2)}) async-start(), calls=%async_computation.5 | async-start | bytes 5529600 | tf_op jit(solution)/shard_map/all_gather | solution.py:57
  7.3 1.2 copy-start.3
  7.3 124.5 %all-gather.11.cloned.1.call-start = ((), (), s32[]{:S(2)}) async-start(), calls=%async_computation.6 | async-start | bytes 1843200 | tf_op jit(solution)/shard_map/all_gather | solution.py:63
  8.0 140.9 %reduce-scatter.4.cloned.1.call-start = ((), (), s32[]{:S(2)}) async-start(), calls=%async_computation.7 | async-start | bytes 884736 | tf_op jit(solution)/shard_map/reduce_scatter | solution.py:66
  134.6 115.0 %all-gather.13.cloned.1.call-start = ((), (), s32[]{:S(2)}) async-start(), calls=%async_computation.8 | async-start | bytes 6635520 | tf_op jit(solution)/shard_map/all_gather | solution.py:76
  135.2 213.5 %all-gather.15.cloned.1.call-start = ((), (), s32[]{:S(2)}) async-start(), calls=%async_computation.9 | async-start | bytes 6635520 | tf_op jit(solution)/shard_map/all_gather | solution.py:80
  135.8 234.9 %reduce-scatter.6.cloned.1.call-start = ((), (), s32[]{:S(2)}) async-start(), calls=%async_computation.10 | async-start | bytes 884736 | tf_op jit(solution)/shard_map/reduce_scatter | solution.py:83
  356.9 13.8 %copy-start.1 = (bf16[256,576]{0,1:T(8,128)(2,1)S(1)}, bf16[256,576]{0,1:T(8,128)(2,1)}, u32[]{:S(2)}) copy-start(bf16[256,576]{0,1:T(8,128)(2,1)} %reduce-scatter.4.cloned.1.call-done) | copy-start | bytes 884740
  356.9 105.9 %all-gather.19.cloned.1.call-start = ((), (), s32[]{:S(2)}) async-start(), calls=%async_computation.12 | async-start | bytes 5529600 | tf_op jit(solution)/shard_map/all_gather | solution.py:119
  357.7 140.5 %all-gather.17.cloned.1.call-start = ((), (), s32[]{:S(2)}) async-start(), calls=%async_computation.11 | async-start | bytes 1843200 | tf_op jit(solution)/shard_map/all_gather | solution.py:113
  358.4 175.7 %all-gather.21.cloned.1.call-start = ((), (), s32[]{:S(2)}) async-start(), calls=%async_computation.13 | async-start | bytes 1843200 | tf_op jit(solution)/shard_map/all_gather | solution.py:126
  371.9 9.6 %copy-start.5 = (s32[4]{0:T(128)S(1)}, s32[4]{0:T(128)}, u32[]{:S(2)}) copy-start(s32[4]{0:T(128)} %param.19) | copy-start | bytes 52
  371.9 9.6 %copy-start.2 = (f32[13,1152]{1,0:T(8,128)S(1)}, f32[13,1152]{1,0:T(8,128)}, u32[]{:S(2)}) copy-start(f32[13,1152]{1,0:T(8,128)} %param.18) | copy-start | bytes 179716
  371.9 9.7 %copy-start.4 = (f32[3,1152]{1,0:T(4,128)S(1)}, f32[3,1152]{1,0:T(4,128)}, u32[]{:S(2)}) copy-start(f32[3,1152]{1,0:T(4,128)} %param.21) | copy-start | bytes 41476
  376.9 92.6 %all-to-all-start = ((bf16[4,2,18432]{2,1,0:T(2,128)(2,1)}), bf16[4,2,18432]{2,1,0:T(2,128)(2,1)S(1)}, u32[]{:S(2)}, u32[]{:S(2)}) async-start(bf16[4,2,18432]{2,1,0:T(2,128)(2,1)} %reshape.175), calls=%async_computation.2 | async-start | bytes 589824 | tf_op jit(solution)/shard_map/all_to_all | solution.py:88
  381.5 166.4 %reduce-scatter.8.cloned.1.call-start = ((), (), s32[]{:S(2)}) async-start(), calls=%async_computation.14 | async-start | bytes 442368 | tf_op jit(solution)/shard_map/reduce_scatter | solution.py:129
Sparse Core Ops, SparseCore 0:
  8.9 87.2 all-gather.8
  97.8 33.9 all-gather.10
  134.8 14.1 reduce-scatter.3
  150.4 99.1 all-gather.12
  251.1 97.4 all-gather.14
  357.0 13.6 reduce-scatter.5
  372.3 90.5 all-gather.18
  464.4 33.6 all-gather.16
  499.7 34.3 all-gather.20
  536.9 10.8 reduce-scatter.7
where the time goes:
time: 557 us
  waiting for transfers between devices  441 us (79%)
  blocking collectives  35.5 us (6%)
  matrix products  32.7 us (6%)
  local copies, waits for them, and re-layouts  20.2 us (4%)
  between operations  13.8 us (2%)
  other arithmetic  7.89 us (1%)
    all_gather x1, waiting for transfers between devices, on_device(): lax.all_gather(w_out, 'seq', axis=2, tiled=True)[0]  99 us
    all_gather x1, waiting for transfers between devices, on_device(): lax.all_gather(w_in, 'seq', axis=1, tiled=True)[0]  89.8 us
    all_gather x1, waiting for transfers between devices, on_device(): piece = lax.all_gather(s_qkv, 'seq', axis=1, tiled=True)  87.6 us
    all_gather x1, waiting for transfers between devices, on_device(): piece = lax.all_gather(t_qkv, 'seq', axis=0, tiled=True)  81.2 us
    all_gather x1, waiting for transfers between devices, on_device(): lax.all_gather(s_out, 'seq', axis=2, tiled=True)[0]  21.4 us
    all_gather x1, waiting for transfers between devices, on_device(): lax.all_gather(t_out, 'seq', axis=1, tiled=True)  17.1 us
    all_gather x1, blocking collectives, on_device(): lax.all_gather(control.astype(jnp.bfloat16), 'mp', axis=2, tiled=True)  16.1 us
    reduce_scatter x1, waiting for transfers between devices, on_device(): lax.psum_scatter(projected.astype(jnp.bfloat16), 'mp', scatter_dimension=...  12.5 us
  transfers between devices with their start and end apart: 11, of which 10 were waited for; matrix products, arithmetic and copies ran while one was open for 8% of the time, Pallas kernels for 0%

commit v1 on v0

--- a/solution.py
+++ b/solution.py
@@ -1,6 +1,10 @@
+import functools
+
 import jax
 import jax.numpy as jnp
 from jax import lax
+from jax.experimental import pallas as pl
+from jax.experimental.pallas import tpu as pltpu
 from jax.sharding import PartitionSpec as P
 
 D = 1152
@@ -132,8 +136,362 @@
     result = joined_share + share(t_mod[2]) * temporal_part
     return result.reshape(frames, positions, quarter)
 
+F32, BF16 = jnp.float32, jnp.bfloat16
+
+
+def dot(left, right):
+    return jnp.dot(left, right, preferred_element_type=F32)
+
+
+def dot_nt(left, right):
+    return lax.dot_general(left, right, (((1,), (1,)), ((), ())), preferred_element_type=F32)
+
+
+def fused_kernel(ring, *refs):
+    n_weights = 7
+    x_ref, mod_ref, gain_ref, tmod_ref = refs[:4]
+    shards = refs[4 : 4 + n_weights]
+    out_ref = refs[4 + n_weights]
+    scratch = refs[5 + n_weights :]
+    bufs = scratch[:n_weights]
+    (qkv_ref, att_ref, x1_ref, send_ref, got_ref, got2_ref, hid_ref, yb_ref, moved_ref,
+     js_ref, jr_ref, ts_ref, tr_ref, tq_ref, ta_ref, jf_ref) = scratch[n_weights : n_weights + 16]
+    local_sem, right_sem, left_sem, z_sem, ysend_sem, y_sem, pair_send, pair_recv, move_send, move_recv = (
+        scratch[n_weights + 16 :]
+    )
+    group, seq, mp, branch = (lax.axis_index(a) for a in ("groups", "seq", "mp", "branch"))
+    depth = shards[0].shape[0]
+    half = depth // 2
+    other = 1 - group
+    quarter = js_ref.shape[1]
+    heads = quarter // HEAD_DIM
+
+    def at(z=None, g=None, m=None, b=None):
+        return (
+            group if g is None else g,
+            seq if z is None else z,
+            mp if m is None else m,
+            branch if b is None else b,
+        )
+
+    def remote(src, dst, send, recv, device):
+        return pltpu.make_async_remote_copy(
+            src_ref=src, dst_ref=dst, send_sem=send, recv_sem=recv,
+            device_id=device, device_id_type=pl.DeviceIdType.MESH,
+        )
+
+    locals_ = []
+    for w in range(n_weights):
+        copy = pltpu.make_async_copy(
+            shards[w], bufs[w].at[pl.ds(seq * depth, depth)], local_sem.at[w]
+        )
+        copy.start()
+        locals_.append(copy)
+
+    partners = [
+        (lax.rem(seq + dz, ring), lax.rem(branch + db, 2))
+        for dz in range(ring)
+        for db in range(2)
+        if dz or db
+    ]
+    barrier = pltpu.get_barrier_semaphore()
+    greeted = [at(z=z, b=b) for z, b in partners] + [at(g=other), at(m=1 - mp)]
+    for device in greeted:
+        pl.semaphore_signal(barrier, inc=1, device_id=device, device_id_type=pl.DeviceIdType.MESH)
+    pl.semaphore_wait(barrier, len(greeted))
+
+    def block(w, s, g):
+        return bufs[w].at[pl.ds(s * depth + g * half, half)]
+
+    def rightward(w, s):
+        ref = block(w, s, group)
+        return remote(ref, ref, right_sem.at[w, s], z_sem.at[w, s], at(z=lax.rem(seq + 1, ring)))
+
+    def leftward(w, s):
+        ref = block(w, s, group)
+        return remote(ref, ref, left_sem.at[w, s], z_sem.at[w, s], at(z=lax.rem(seq + ring - 1, ring)))
+
+    def across(w, s, g):
+        ref = block(w, s, g)
+        return remote(ref, ref, ysend_sem.at[w, s], y_sem.at[w, s], at(g=other))
+
+    def own(w):
+        locals_[w].wait()
+
+        @pl.when(seq < ring - 1)
+        def _():
+            rightward(w, seq).start()
+
+        @pl.when(seq > 0)
+        def _():
+            leftward(w, seq).start()
+
+    def step(w, d):
+        @pl.when(seq - d >= 0)
+        def _():
+            s = seq - d
+            rightward(w, s).wait_recv()
+
+            @pl.when(seq < ring - 1)
+            def _():
+                rightward(w, s).start()
+
+            across(w, s, group).start()
+
+        @pl.when(seq + d < ring)
+        def _():
+            s = seq + d
+            leftward(w, s).wait_recv()
+
+            @pl.when(seq > 0)
+            def _():
+                leftward(w, s).start()
+
+            across(w, s, group).start()
+
+    def finish(w):
+        for d in range(1, ring):
+
+            @pl.when(seq - d >= 0)
+            def _():
+                across(w, seq - d, other).wait_recv()
+
+            @pl.when(seq + d < ring)
+            def _():
+                across(w, seq + d, other).wait_recv()
+
+    def drain(w):
+        @pl.when(seq < ring - 1)
+        def _():
+            rightward(w, seq).wait_send()
+
+        @pl.when(seq > 0)
+        def _():
+            leftward(w, seq).wait_send()
+
+        for d in range(1, ring):
+
+            @pl.when(seq - d >= 0)
+            def _():
+                across(w, seq - d, group).wait_send()
+
+                @pl.when(seq < ring - 1)
+                def _():
+                    rightward(w, seq - d).wait_send()
+
+            @pl.when(seq + d < ring)
+            def _():
+                across(w, seq + d, group).wait_send()
+
+                @pl.when(seq > 0)
+                def _():
+                    leftward(w, seq + d).wait_send()
+
+    def pair(i, src, dst):
+        return remote(src, dst, pair_send.at[i], pair_recv.at[i], at(m=1 - mp))
+
+    scale = 1.0 / (HEAD_DIM**0.5)
+    own(0)
+    own(1)
+    normed = layer_norm(x_ref[...], mod_ref[0:1], mod_ref[1:2]).astype(BF16)
+    step(0, 1)
+    own(2)
+    for d in range(2, ring):
+        step(0, d)
+    step(1, 1)
+    own(3)
+    for d in range(2, ring):
+        step(1, d)
+    finish(0)
+    qkv_ref[...] = dot(normed, bufs[0][...])
+    for i in range(heads):
+        lo = i * HEAD_DIM
+        query = (qkv_ref[:, lo : lo + HEAD_DIM] * scale).astype(BF16)
+        keys = qkv_ref[:, quarter + lo : quarter + lo + HEAD_DIM].astype(BF16)
+        values = qkv_ref[:, 2 * quarter + lo : 2 * quarter + lo + HEAD_DIM].astype(BF16)
+        weights = jnp.exp(dot_nt(query, keys))
+        total = jnp.sum(weights, axis=-1, keepdims=True)
+        att_ref[:, lo : lo + HEAD_DIM] = dot(weights.astype(BF16), values) / total
+    finish(1)
+    projected = dot_nt(att_ref[...].astype(BF16), bufs[1][...])
+    send_ref[0] = projected.astype(BF16)
+    pair0 = pair(0, send_ref.at[0], got_ref)
+    pair0.start()
+    x1_ref[...] = x_ref[...] + mod_ref[2:3] * projected
+    step(2, 1)
+    own(4)
+    step(2, 2) if ring > 2 else None
+    pair0.wait_recv()
+    x1_ref[...] += mod_ref[2:3] * got_ref[...].astype(F32)
+    normed = layer_norm(x1_ref[...], mod_ref[3:4], mod_ref[4:5]).astype(BF16)
+    for d in range(3, ring):
+        step(2, d)
+    step(3, 1)
+    own(5)
+    finish(2)
+    send_ref[1] = normed
+    wide = bufs[2].shape[1]
+    tile = 768 if wide % 768 == 0 else wide
+
+    def up(c, _):
+        cols = pl.ds(pl.multiple_of(c * tile, tile), tile)
+        hid_ref[:, cols] = jax.nn.gelu(dot(send_ref[1], bufs[2][:, cols]), approximate=True).astype(BF16)
+        return 0
+
+    lax.fori_loop(0, wide // tile, up, 0)
+    for d in range(2, ring):
+        step(3, d)
+    own(6)
+    step(4, 1)
+    finish(3)
+    down = dot_nt(hid_ref[...], bufs[3][...])
+    send_ref[2] = down.astype(BF16)
+    pair1 = pair(1, send_ref.at[2], got2_ref)
+    pair1.start()
+    x1_ref[...] += mod_ref[5:6] * down
+    for d in range(2, ring):
+        step(4, d)
+    step(5, 1)
+    pair1.wait_recv()
+    yb_ref[...] = (x1_ref[...] + mod_ref[5:6] * got2_ref[...].astype(F32)).astype(BF16)
+    positions = moved_ref.shape[2]
+
+    def rows_of(z, b):
+        return pl.ds(pl.multiple_of((z * 2 + b) * positions, positions), positions)
+
+    sends = []
+    for i, (z, b) in enumerate(partners):
+        copy = remote(
+            yb_ref.at[rows_of(z, b)], moved_ref.at[branch, seq],
+            move_send.at[i], move_recv.at[branch, seq], at(z=z, b=b),
+        )
+        copy.start()
+        sends.append(copy)
+    moved_ref[branch, seq] = yb_ref[rows_of(seq, branch), :]
+    for d in range(2, ring):
+        step(5, d)
+    step(6, 1)
+    for z, b in partners:
+        remote(
+            yb_ref.at[rows_of(seq, branch)], moved_ref.at[b, z],
+            move_send.at[0], move_recv.at[b, z], at(z=z, b=b),
+        ).wait_recv()
+    finish(4)
+    rows = ring * positions
+    hint_in = (moved_ref[0].astype(F32) * gain_ref[...][:, None, :]).astype(BF16)
+    hint = dot(hint_in.reshape(rows, D), bufs[4][...])
+    main = moved_ref[1].astype(F32).reshape(rows, D)
+    first = mp == 0
+
+    def share(value):
+        return jnp.where(first, value[:, :quarter], value[:, quarter:])
+
+    joined_share = share(main) + hint
+    js_ref[...] = joined_share.astype(BF16)
+    pair2 = pair(2, js_ref, jr_ref)
+    pair2.start()
+    for d in range(2, ring):
+        step(6, d)
+    finish(5)
+    pair2.wait_recv()
+    mine, theirs = joined_share, jr_ref[...].astype(F32)
+    jf_ref[:, :quarter] = jnp.where(first, mine, theirs)
+    jf_ref[:, quarter:] = jnp.where(first, theirs, mine)
+    normed = layer_norm(jf_ref[...], tmod_ref[0:1], tmod_ref[1:2]).astype(BF16)
+    tq_ref[...] = dot(normed, bufs[5][...])
+    place = lax.rem(lax.broadcasted_iota(jnp.int32, (rows, rows), 0), positions)
+    place_k = lax.rem(lax.broadcasted_iota(jnp.int32, (rows, rows), 1), positions)
+    same = place == place_k
+    for i in range(heads):
+        lo = i * HEAD_DIM
+        query = (tq_ref[:, lo : lo + HEAD_DIM] * scale).astype(BF16)
+        keys = tq_ref[:, quarter + lo : quarter + lo + HEAD_DIM].astype(BF16)
+        values = tq_ref[:, 2 * quarter + lo : 2 * quarter + lo + HEAD_DIM].astype(BF16)
+        weights = jnp.where(same, jnp.exp(dot_nt(query, keys)), 0.0)
+        total = jnp.sum(weights, axis=-1, keepdims=True)
+        ta_ref[:, lo : lo + HEAD_DIM] = dot(weights.astype(BF16), values) / total
+    finish(6)
+    projected = dot_nt(ta_ref[...].astype(BF16), bufs[6][...])
+    ts_ref[...] = jnp.where(first, projected[:, quarter:], projected[:, :quarter]).astype(BF16)
+    pair3 = pair(3, ts_ref, tr_ref)
+    pair3.start()
+    for w in range(n_weights):
+        drain(w)
+    for copy in sends:
+        copy.wait_send()
+    pair3.wait_recv()
+    gate = share(tmod_ref[2:3])
+    out_ref[...] = joined_share + gate * (share(projected) + tr_ref[...].astype(F32))
+    for copy in (pair0, pair1, pair2, pair3):
+        copy.wait_send()
+
+
+def fused(
+    streams, modulation, s_qkv, s_out, w_in, w_out, hint_gain, inject_layer, hint_weight, t_mod, t_qkv, t_out
+):
+    ring = inject_layer.shape[0]
+    tokens, quarter = streams.shape[2], s_qkv.shape[3]
+    positions = tokens // (2 * ring)
+    rows = ring * positions
+    gain = hint_gain[inject_layer]
+    depth = s_qkv.shape[1]
+    shards = [
+        s_qkv[0].reshape(depth, 3 * quarter),
+        s_out[0].T,
+        w_in[0],
+        w_out[0].T,
+        hint_weight,
+        t_qkv.reshape(depth, 3 * quarter),
+        t_out.T,
+    ]
+    n = len(shards)
+    dma = pltpu.SemaphoreType.DMA
+    vmem = pl.BlockSpec(memory_space=pltpu.VMEM)
+    anywhere = pl.BlockSpec(memory_space=pl.ANY)
+    out = pl.pallas_call(
+        functools.partial(fused_kernel, ring),
+        out_shape=jax.ShapeDtypeStruct((rows, quarter), F32),
+        in_specs=[vmem] * 4 + [anywhere] * n,
+        out_specs=vmem,
+        scratch_shapes=[pltpu.VMEM((ring * depth, a.shape[1]), BF16) for a in shards]
+        + [
+            pltpu.VMEM((tokens, 3 * quarter), F32),
+            pltpu.VMEM((tokens, quarter), F32),
+            pltpu.VMEM((tokens, D), F32),
+            pltpu.VMEM((3, tokens, D), BF16),
+            pltpu.VMEM((tokens, D), BF16),
+            pltpu.VMEM((tokens, D), BF16),
+            pltpu.VMEM((tokens, w_in.shape[2]), BF16),
+            pltpu.VMEM((tokens, D), BF16),
+            pltpu.VMEM((2, ring, positions, D), BF16),
+            pltpu.VMEM((rows, quarter), BF16),
+            pltpu.VMEM((rows, quarter), BF16),
+            pltpu.VMEM((rows, quarter), BF16),
+            pltpu.VMEM((rows, quarter), BF16),
+            pltpu.VMEM((rows, 3 * quarter), F32),
+            pltpu.VMEM((rows, quarter), F32),
+            pltpu.VMEM((rows, D), F32),
+            dma((n,)),
+            dma((n, ring)),
+            dma((n, ring)),
+            dma((n, ring)),
+            dma((n, ring)),
+            dma((n, ring)),
+            dma((4,)),
+            dma((4,)),
+            dma((2 * ring - 1,)),
+            dma((2, ring)),
+        ],
+        compiler_params=pltpu.CompilerParams(
+            collective_id=0, has_side_effects=True, vmem_limit_bytes=50 * 1024 * 1024
+        ),
+    )(streams[0, 0], modulation[0], gain, t_mod, *shards)
+    return out.reshape(ring, positions, quarter)
+
 
 def solution(mesh):
+    sizes = dict(mesh.shape)
+    fits = (sizes["groups"], sizes["mp"], sizes["branch"]) == (2, 2, 2) and sizes["seq"] in (2, 4)
     in_specs = (
         P("branch", ("groups", "seq"), None, None),
         P("branch", None, None),
@@ -150,5 +508,5 @@
     )
     out_specs = P("groups", ("seq", "branch"), "mp")
     return jax.shard_map(
-        on_device, mesh=mesh, in_specs=in_specs, out_specs=out_specs, check_vma=False
-    )
+        fused if fits else on_device, mesh=mesh, in_specs=in_specs, out_specs=out_specs, check_vma=False
+    )

time: 557 us -> 248 us (0.45)
  waiting for transfers between devices: 441 us -> 0 us
  Pallas kernels: 0 us -> 239 us
  blocking collectives: 35.5 us -> 0 us
  matrix products: 32.7 us -> 0 us
  between operations: 13.8 us -> 0.15 us
  local copies, waits for them, and re-layouts: 20.2 us -> 8.41 us
  other arithmetic: 7.89 us -> 0.01 us
    all_gather x7 -> x0, waiting for transfers between devices: 402 us -> none  [the longest x1 99 us: on_device(): lax.all_gather(w_out, 'seq', axis=2, tiled=True)[0]]
    pallas_call x0 -> x1, Pallas kernels: none -> 239 us  [fused(): pl.pallas_call(functools.partial(fused_kernel, ring), out_shape=jax.Shape...]
    reduce_scatter x3 -> x0, waiting for transfers between devices: 34.9 us -> none  [the longest x1 12.5 us: on_device(): lax.psum_scatter(projected.astype(jnp.bfloat16), 'mp', scatter_dimension=...]
    dot_general x10 -> x0, matrix products: 32.7 us -> none  [the longest x3 10.1 us: row_product(): return jnp.dot(left, piece, preferred_element_type=jnp.float32)]
    all_gather x3 -> x0, blocking collectives: 31.5 us -> none  [the longest x1 16.1 us: on_device(): lax.all_gather(control.astype(jnp.bfloat16), 'mp', axis=2, tiled=True)]
    all_gather x3 -> x0, local copies, waits for them, and re-layouts: 14.3 us -> none  [the longest x1 6.58 us: on_device(): piece = lax.all_gather(s_qkv, 'seq', axis=1, tiled=True)]
  transfers between devices with their start and end apart: 11 -> 0, of which waited for: 10 -> 0; matrix products, arithmetic and copies ran while one was open for 8% -> 0% of each run, Pallas kernels for 0% -> 0%
where the time goes in v1:
time: 248 us
  Pallas kernels  239 us (96%)
  local copies, waits for them, and re-layouts  8.41 us (3%)
    pallas_call x1, Pallas kernels, fused(): pl.pallas_call(functools.partial(fused_kernel, ring), out_shape=jax.Shape...  239 us

profile of v1, /device:TPU:0, one launch (start us, length us, event | category | flops | bytes accessed | tf_op | source)
XLA Modules:
  0.0 247.6 jit_solution(10944835268710545219)
XLA Ops:
  0.0 0.0 copy-start
  0.0 2.0 copy.15
  2.0 0.0 copy-start.5
  2.0 1.7 copy.17.refs_4_
  3.7 0.0 copy-done.5
  3.7 1.6 copy.16
  5.3 0.0 copy-start.6
  5.3 0.0 copy-start.7
  5.3 0.0 copy-start.1
  5.3 0.0 copy-start.2
  5.3 0.0 copy-start.3
  5.3 0.0 copy-start.4
  5.3 1.8 copy.18.refs_9_
  7.2 0.0 copy-done.6
  7.2 0.0 copy-done.7
  7.2 0.0 copy-done
  7.2 0.6 gather_fusion
  7.8 0.0 copy-done.1
  7.8 0.0 copy-done.2
  7.8 0.0 copy-done.3
  7.8 0.0 copy-done.4
  7.8 239.0 %shard_map.118 = f32[128,576]{1,0:T(8,128)S(1)} custom-call(f32[256,1152]{1,0:T(8,128)} %bitcast.23, f32[6,1152]{1,0:T(8,128)S(1)} %bitcast.18, f32[4,1152]{1,0:T(4,128)S(1)} %gather_fusion, f32[3,1152]{1,0:T(4,128)S(1)} %copy-done.4, bf16[288,1728]{1,0:T(8,128)(2,1)S(1)} %copy.17.refs_4_, bf16[288,576]{1,0:T(8,128)(2,1)S(1)} %bitcast.16, ...), custom_call_target="tpu_custom_call" | custom-call | tf_op jit(solution)/shard_map/pallas_call | solution.py:451
  246.9 0.7 copy.23
  (3 shorter events, 0.0 us)
Async XLA Ops:
  0.0 7.2 %copy-start = (f32[13,1152]{1,0:T(8,128)S(1)}, f32[13,1152]{1,0:T(8,128)}, u32[]{:S(2)}) copy-start(f32[13,1152]{1,0:T(8,128)} %param.18) | copy-start | bytes 179716
  2.0 1.7 copy-start.5
  5.3 1.8 copy-start.6
  5.3 1.9 copy-start.7
  5.3 2.5 %copy-start.1 = (bf16[1,576,288]{1,2,0:T(8,128)(2,1)S(1)}, bf16[1,576,288]{1,2,0:T(8,128)(2,1)}, u32[]{:S(2)}) copy-start(bf16[1,576,288]{1,2,0:T(8,128)(2,1)} %param.15) | copy-start | bytes 995332
  5.3 2.5 %copy-start.2 = (bf16[288,576]{1,0:T(8,128)(2,1)S(1)}, bf16[288,576]{1,0:T(8,128)(2,1)}, u32[]{:S(2)}) copy-start(bf16[288,576]{1,0:T(8,128)(2,1)} %refs_8_.1) | copy-start | bytes 995332
  5.3 2.5 %copy-start.3 = (bf16[576,288]{0,1:T(8,128)(2,1)S(1)}, bf16[576,288]{0,1:T(8,128)(2,1)}, u32[]{:S(2)}) copy-start(bf16[576,288]{0,1:T(8,128)(2,1)} %param.23) | copy-start | bytes 995332
  5.3 2.5 %copy-start.4 = (f32[3,1152]{1,0:T(4,128)S(1)}, f32[3,1152]{1,0:T(4,128)}, u32[]{:S(2)}) copy-start(f32[3,1152]{1,0:T(4,128)} %refs_3_.1) | copy-start | bytes 41476

commit v2 on v1

--- a/solution.py
+++ b/solution.py
@@ -148,7 +148,7 @@
 
 
 def fused_kernel(ring, *refs):
-    n_weights = 7
+    n_weights = 6
     x_ref, mod_ref, gain_ref, tmod_ref = refs[:4]
     shards = refs[4 : 4 + n_weights]
     out_ref = refs[4 + n_weights]
@@ -156,7 +156,7 @@
     bufs = scratch[:n_weights]
     (qkv_ref, att_ref, x1_ref, send_ref, got_ref, got2_ref, hid_ref, yb_ref, moved_ref,
      js_ref, jr_ref, ts_ref, tr_ref, tq_ref, ta_ref, jf_ref) = scratch[n_weights : n_weights + 16]
-    local_sem, right_sem, left_sem, z_sem, ysend_sem, y_sem, pair_send, pair_recv, move_send, move_recv = (
+    local_sem, right_sem, left_sem, z_sem, ysend_sem, y_sem, pair_send, pair_recv, move_send, move_recv, core_send, core_recv = (
         scratch[n_weights + 16 :]
     )
     group, seq, mp, branch = (lax.axis_index(a) for a in ("groups", "seq", "mp", "branch"))
@@ -180,10 +180,13 @@
             device_id=device, device_id_type=pl.DeviceIdType.MESH,
         )
 
+    shared = 4
     locals_ = []
     for w in range(n_weights):
         copy = pltpu.make_async_copy(
-            shards[w], bufs[w].at[pl.ds(seq * depth, depth)], local_sem.at[w]
+            shards[w],
+            bufs[w].at[:, pl.ds(seq * depth, depth)] if w == shared else bufs[w].at[pl.ds(seq * depth, depth)],
+            local_sem.at[w],
         )
         copy.start()
         locals_.append(copy)
@@ -201,7 +204,17 @@
     pl.semaphore_wait(barrier, len(greeted))
 
     def block(w, s, g):
-        return bufs[w].at[pl.ds(s * depth + g * half, half)]
+        rows = pl.ds(s * depth + g * half, half)
+        return bufs[w].at[branch, rows] if w == shared else bufs[w].at[rows]
+
+    def over(kind, s):
+        ref = block(shared, s, other if kind else group)
+        return remote(ref, ref, core_send.at[kind, s], core_recv.at[kind, s], at(b=1 - branch))
+
+    def over_wait(kind, s):
+        g = other if kind else group
+        ref = bufs[shared].at[1 - branch, pl.ds(s * depth + g * half, half)]
+        remote(ref, ref, core_send.at[kind, s], core_recv.at[kind, s], at(b=1 - branch)).wait_recv()
 
     def rightward(w, s):
         ref = block(w, s, group)
@@ -237,6 +250,8 @@
                 rightward(w, s).start()
 
             across(w, s, group).start()
+            if w == shared:
+                over(0, s).start()
 
         @pl.when(seq + d < ring)
         def _():
@@ -248,17 +263,30 @@
                 leftward(w, s).start()
 
             across(w, s, group).start()
+            if w == shared:
+                over(0, s).start()
 
     def finish(w):
         for d in range(1, ring):
 
-            @pl.when(seq - d >= 0)
-            def _():
-                across(w, seq - d, other).wait_recv()
-
-            @pl.when(seq + d < ring)
-            def _():
-                across(w, seq + d, other).wait_recv()
+            for sign in (-1, 1):
+                s = seq + sign * d
+
+                @pl.when((s >= 0) & (s < ring))
+                def _():
+                    across(w, s, other).wait_recv()
+                    if w == shared:
+                        over(1, s).start()
+
+    def finish_shared():
+        for d in range(1, ring):
+            for sign in (-1, 1):
+                s = seq + sign * d
+
+                @pl.when((s >= 0) & (s < ring))
+                def _():
+                    over_wait(0, s)
+                    over_wait(1, s)
 
     def drain(w):
         @pl.when(seq < ring - 1)
@@ -274,6 +302,9 @@
             @pl.when(seq - d >= 0)
             def _():
                 across(w, seq - d, group).wait_send()
+                if w == shared:
+                    over(0, seq - d).wait_send()
+                    over(1, seq - d).wait_send()
 
                 @pl.when(seq < ring - 1)
                 def _():
@@ -282,6 +313,9 @@
             @pl.when(seq + d < ring)
             def _():
                 across(w, seq + d, group).wait_send()
+                if w == shared:
+                    over(0, seq + d).wait_send()
+                    over(1, seq + d).wait_send()
 
                 @pl.when(seq > 0)
                 def _():
@@ -312,14 +346,15 @@
         weights = jnp.exp(dot_nt(query, keys))
         total = jnp.sum(weights, axis=-1, keepdims=True)
         att_ref[:, lo : lo + HEAD_DIM] = dot(weights.astype(BF16), values) / total
+        if i == heads // 2:
+            step(2, 1)
+            own(4)
     finish(1)
     projected = dot_nt(att_ref[...].astype(BF16), bufs[1][...])
     send_ref[0] = projected.astype(BF16)
     pair0 = pair(0, send_ref.at[0], got_ref)
     pair0.start()
     x1_ref[...] = x_ref[...] + mod_ref[2:3] * projected
-    step(2, 1)
-    own(4)
     step(2, 2) if ring > 2 else None
     pair0.wait_recv()
     x1_ref[...] += mod_ref[2:3] * got_ref[...].astype(F32)
@@ -341,7 +376,6 @@
     lax.fori_loop(0, wide // tile, up, 0)
     for d in range(2, ring):
         step(3, d)
-    own(6)
     step(4, 1)
     finish(3)
     down = dot_nt(hid_ref[...], bufs[3][...])
@@ -370,16 +404,16 @@
     moved_ref[branch, seq] = yb_ref[rows_of(seq, branch), :]
     for d in range(2, ring):
         step(5, d)
-    step(6, 1)
+    finish(4)
     for z, b in partners:
         remote(
             yb_ref.at[rows_of(seq, branch)], moved_ref.at[b, z],
             move_send.at[0], move_recv.at[b, z], at(z=z, b=b),
         ).wait_recv()
-    finish(4)
+    finish_shared()
     rows = ring * positions
     hint_in = (moved_ref[0].astype(F32) * gain_ref[...][:, None, :]).astype(BF16)
-    hint = dot(hint_in.reshape(rows, D), bufs[4][...])
+    hint = dot(hint_in.reshape(rows, D), bufs[4][1, :, quarter:])
     main = moved_ref[1].astype(F32).reshape(rows, D)
     first = mp == 0
 
@@ -390,15 +424,13 @@
     js_ref[...] = joined_share.astype(BF16)
     pair2 = pair(2, js_ref, jr_ref)
     pair2.start()
-    for d in range(2, ring):
-        step(6, d)
-    finish(5)
     pair2.wait_recv()
     mine, theirs = joined_share, jr_ref[...].astype(F32)
     jf_ref[:, :quarter] = jnp.where(first, mine, theirs)
     jf_ref[:, quarter:] = jnp.where(first, theirs, mine)
     normed = layer_norm(jf_ref[...], tmod_ref[0:1], tmod_ref[1:2]).astype(BF16)
-    tq_ref[...] = dot(normed, bufs[5][...])
+    tq_ref[:, : 2 * quarter] = dot(normed, bufs[4][0])
+    tq_ref[:, 2 * quarter :] = dot(normed, bufs[4][1, :, :quarter])
     place = lax.rem(lax.broadcasted_iota(jnp.int32, (rows, rows), 0), positions)
     place_k = lax.rem(lax.broadcasted_iota(jnp.int32, (rows, rows), 1), positions)
     same = place == place_k
@@ -410,8 +442,8 @@
         weights = jnp.where(same, jnp.exp(dot_nt(query, keys)), 0.0)
         total = jnp.sum(weights, axis=-1, keepdims=True)
         ta_ref[:, lo : lo + HEAD_DIM] = dot(weights.astype(BF16), values) / total
-    finish(6)
-    projected = dot_nt(ta_ref[...].astype(BF16), bufs[6][...])
+    finish(5)
+    projected = dot_nt(ta_ref[...].astype(BF16), bufs[5][...])
     ts_ref[...] = jnp.where(first, projected[:, quarter:], projected[:, :quarter]).astype(BF16)
     pair3 = pair(3, ts_ref, tr_ref)
     pair3.start()
@@ -440,8 +472,9 @@
         s_out[0].T,
         w_in[0],
         w_out[0].T,
-        hint_weight,
-        t_qkv.reshape(depth, 3 * quarter),
+        jnp.concatenate([t_qkv.reshape(depth, 3 * quarter), hint_weight], axis=1)
+        .reshape(depth, 2, 2 * quarter)
+        .transpose(1, 0, 2),
         t_out.T,
     ]
     n = len(shards)
@@ -453,7 +486,7 @@
         out_shape=jax.ShapeDtypeStruct((rows, quarter), F32),
         in_specs=[vmem] * 4 + [anywhere] * n,
         out_specs=vmem,
-        scratch_shapes=[pltpu.VMEM((ring * depth, a.shape[1]), BF16) for a in shards]
+        scratch_shapes=[pltpu.VMEM(a.shape[:-2] + (ring * depth, a.shape[-1]), BF16) for a in shards]
         + [
             pltpu.VMEM((tokens, 3 * quarter), F32),
             pltpu.VMEM((tokens, quarter), F32),
@@ -481,6 +514,8 @@
             dma((4,)),
             dma((2 * ring - 1,)),
             dma((2, ring)),
+            dma((2, ring)),
+            dma((2, ring)),
         ],
         compiler_params=pltpu.CompilerParams(
             collective_id=0, has_side_effects=True, vmem_limit_bytes=50 * 1024 * 1024

time: 248 us -> 226 us (0.911)
  Pallas kernels: 239 us -> 216 us
    pallas_call x1, Pallas kernels: 239 us -> 216 us  [fused(): pl.pallas_call(functools.partial(fused_kernel, ring), out_shape=jax.Shape...]
    unnamed x20 -> x23, local copies, waits for them, and re-layouts: 4.38 us -> 5.36 us
where the time goes in v2:
time: 226 us
  Pallas kernels  216 us (96%)
  local copies, waits for them, and re-layouts  9.39 us (4%)
    pallas_call x1, Pallas kernels, fused(): pl.pallas_call(functools.partial(fused_kernel, ring), out_shape=jax.Shape...  216 us
    unnamed x23, local copies, waits for them, and re-layouts  5.36 us

profile of v2, /device:TPU:0, one launch (start us, length us, event | category | flops | bytes accessed | tf_op | source)
XLA Modules:
  0.0 226.3 jit_solution(9214656067267074854)
XLA Ops:
  0.0 0.0 copy-start
  0.0 0.0 copy-start.6
  0.0 2.0 copy.15
  2.0 0.0 copy-done.6
  2.1 1.0 copy.16
  3.0 1.2 pad_maximum_fusion
  4.2 0.0 copy-start.5
  4.2 1.6 copy.18
  5.9 0.0 copy-done.5
  5.9 1.6 copy.14
  7.5 0.0 copy-start.7
  7.5 0.0 copy-start.8
  7.5 0.0 copy-start.1
  7.5 0.0 copy-start.2
  7.5 0.0 copy-start.3
  7.5 0.0 copy-start.4
  7.5 1.8 copy.19.refs_4_
  9.3 0.0 copy-done.7
  9.4 0.0 copy-done.8
  9.4 0.0 copy-done
  9.4 0.6 gather_fusion
  10.0 0.0 copy-done.1
  10.0 0.0 copy-done.2
  10.0 0.0 copy-done.3
  10.0 0.0 copy-done.4
  10.0 215.6 %shard_map.118 = f32[128,576]{1,0:T(8,128)S(1)} custom-call(f32[256,1152]{1,0:T(8,128)S(1)} %bitcast.18, f32[6,1152]{1,0:T(8,128)S(1)} %bitcast.21, f32[4,1152]{1,0:T(4,128)S(1)} %gather_fusion, f32[3,1152]{1,0:T(4,128)S(1)} %copy-done.4, bf16[288,1728]{1,0:T(8,128)(2,1)S(1)} %copy.19.refs_4_, bf16[288,576]{1,0:T(8,128)(2,1)S(1)} %bitcast.19, ...), custom_call_target="tpu_custom_call" | custom-call | tf_op jit(solution)/shard_map/pallas_call | solution.py:484
  225.6 0.7 copy.26
  (3 shorter events, 0.0 us)
Async XLA Ops:
  0.0 9.4 %copy-start = (f32[13,1152]{1,0:T(8,128)S(1)}, f32[13,1152]{1,0:T(8,128)}, u32[]{:S(2)}) copy-start(f32[13,1152]{1,0:T(8,128)} %param.18) | copy-start | bytes 179716
  0.0 2.0 copy-start.6
  4.2 1.6 copy-start.5
  7.5 1.9 copy-start.7
  7.5 1.9 copy-start.8
  7.5 2.5 %copy-start.1 = (f32[1,1,256,1152]{3,2,1,0:T(8,128)S(1)}, f32[1,1,256,1152]{3,2,1,0:T(8,128)}, u32[]{:S(2)}) copy-start(f32[1,1,256,1152]{3,2,1,0:T(8,128)} %param.12) | copy-start | bytes 3538948
  7.5 2.5 %copy-start.2 = (bf16[1,576,288]{1,2,0:T(8,128)(2,1)S(1)}, bf16[1,576,288]{1,2,0:T(8,128)(2,1)}, u32[]{:S(2)}) copy-start(bf16[1,576,288]{1,2,0:T(8,128)(2,1)} %param.15) | copy-start | bytes 995332
  7.5 2.5 %copy-start.3 = (bf16[576,288]{0,1:T(8,128)(2,1)S(1)}, bf16[576,288]{0,1:T(8,128)(2,1)}, u32[]{:S(2)}) copy-start(bf16[576,288]{0,1:T(8,128)(2,1)} %param.23) | copy-start | bytes 995332
  7.5 2.5 %copy-start.4 = (f32[3,1152]{1,0:T(4,128)S(1)}, f32[3,1152]{1,0:T(4,128)}, u32[]{:S(2)}) copy-start(f32[3,1152]{1,0:T(4,128)} %refs_3_.1) | copy-start | bytes 41476

commit v3 on v2

--- a/solution.py
+++ b/solution.py
@@ -327,13 +327,14 @@
     scale = 1.0 / (HEAD_DIM**0.5)
     own(0)
     own(1)
+    own(2)
     normed = layer_norm(x_ref[...], mod_ref[0:1], mod_ref[1:2]).astype(BF16)
     step(0, 1)
-    own(2)
+    own(3)
     for d in range(2, ring):
         step(0, d)
     step(1, 1)
-    own(3)
+    own(4)
     for d in range(2, ring):
         step(1, d)
     finish(0)
@@ -348,7 +349,7 @@
         att_ref[:, lo : lo + HEAD_DIM] = dot(weights.astype(BF16), values) / total
         if i == heads // 2:
             step(2, 1)
-            own(4)
+            own(5)
     finish(1)
     projected = dot_nt(att_ref[...].astype(BF16), bufs[1][...])
     send_ref[0] = projected.astype(BF16)
@@ -362,7 +363,6 @@
     for d in range(3, ring):
         step(2, d)
     step(3, 1)
-    own(5)
     finish(2)
     send_ref[1] = normed
     wide = bufs[2].shape[1]

time: 226 us -> 234 us (1.035)
  Pallas kernels: 216 us -> 223 us
    pallas_call x1, Pallas kernels: 216 us -> 223 us  [fused(): pl.pallas_call(functools.partial(fused_kernel, ring), out_shape=jax.Shape...]
where the time goes in v3:
time: 234 us
  Pallas kernels  223 us (95%)
  local copies, waits for them, and re-layouts  9.39 us (4%)
    pallas_call x1, Pallas kernels, fused(): pl.pallas_call(functools.partial(fused_kernel, ring), out_shape=jax.Shape...  223 us
    unnamed x23, local copies, waits for them, and re-layouts  5.36 us

profile of v3, /device:TPU:0, one launch (start us, length us, event | category | flops | bytes accessed | tf_op | source)
XLA Modules:
  0.0 234.2 jit_solution(6680028527990261202)
XLA Ops:
  0.0 0.0 copy-start
  0.0 0.0 copy-start.6
  0.0 2.0 copy.15
  2.0 0.0 copy-done.6
  2.1 1.0 copy.16
  3.0 1.2 pad_maximum_fusion
  4.2 0.0 copy-start.5
  4.2 1.6 copy.18
  5.9 0.0 copy-done.5
  5.9 1.6 copy.14
  7.5 0.0 copy-start.7
  7.5 0.0 copy-start.8
  7.5 0.0 copy-start.1
  7.5 0.0 copy-start.2
  7.5 0.0 copy-start.3
  7.5 0.0 copy-start.4
  7.5 1.8 copy.19.refs_4_
  9.3 0.0 copy-done.7
  9.4 0.0 copy-done.8
  9.4 0.0 copy-done
  9.4 0.6 gather_fusion
  10.0 0.0 copy-done.1
  10.0 0.0 copy-done.2
  10.0 0.0 copy-done.3
  10.0 0.0 copy-done.4
  10.0 223.5 %shard_map.118 = f32[128,576]{1,0:T(8,128)S(1)} custom-call(f32[256,1152]{1,0:T(8,128)S(1)} %bitcast.18, f32[6,1152]{1,0:T(8,128)S(1)} %bitcast.21, f32[4,1152]{1,0:T(4,128)S(1)} %gather_fusion, f32[3,1152]{1,0:T(4,128)S(1)} %copy-done.4, bf16[288,1728]{1,0:T(8,128)(2,1)S(1)} %copy.19.refs_4_, bf16[288,576]{1,0:T(8,128)(2,1)S(1)} %bitcast.19, ...), custom_call_target="tpu_custom_call" | custom-call | tf_op jit(solution)/shard_map/pallas_call | solution.py:484
  233.5 0.7 copy.26
  (3 shorter events, 0.0 us)
Async XLA Ops:
  0.0 9.4 %copy-start = (f32[13,1152]{1,0:T(8,128)S(1)}, f32[13,1152]{1,0:T(8,128)}, u32[]{:S(2)}) copy-start(f32[13,1152]{1,0:T(8,128)} %param.18) | copy-start | bytes 179716
  0.0 2.0 copy-start.6
  4.2 1.6 copy-start.5
  7.5 1.9 copy-start.7
  7.5 1.9 copy-start.8
  7.5 2.5 %copy-start.1 = (f32[1,1,256,1152]{3,2,1,0:T(8,128)S(1)}, f32[1,1,256,1152]{3,2,1,0:T(8,128)}, u32[]{:S(2)}) copy-start(f32[1,1,256,1152]{3,2,1,0:T(8,128)} %param.12) | copy-start | bytes 3538948
  7.5 2.5 %copy-start.2 = (bf16[1,576,288]{1,2,0:T(8,128)(2,1)S(1)}, bf16[1,576,288]{1,2,0:T(8,128)(2,1)}, u32[]{:S(2)}) copy-start(bf16[1,576,288]{1,2,0:T(8,128)(2,1)} %param.15) | copy-start | bytes 995332
  7.5 2.5 %copy-start.3 = (bf16[576,288]{0,1:T(8,128)(2,1)S(1)}, bf16[576,288]{0,1:T(8,128)(2,1)}, u32[]{:S(2)}) copy-start(bf16[576,288]{0,1:T(8,128)(2,1)} %param.23) | copy-start | bytes 995332
  7.5 2.5 %copy-start.4 = (f32[3,1152]{1,0:T(4,128)S(1)}, f32[3,1152]{1,0:T(4,128)}, u32[]{:S(2)}) copy-start(f32[3,1152]{1,0:T(4,128)} %refs_3_.1) | copy-start | bytes 41476
